TPU v7x, 32 devices: a whole 2x2x4 slice. The times are simulated.
32 devices in a mesh: row: 16 (over z, y, x), col: 2 (over core).
Axes of the slice: x: 2, y: 2, z: 4, core: 2. Of those that a mesh axis runs over, the one named last changes fastest.
Arguments:
- start_vectors: float32 [8192, 128], P(('row', 'col')), may hold values from -6 to 6
- tiles: bfloat16 [16, 2, 2, 512, 512], P('row', 'col'), may hold values from -0.25 to 0.25
- tile_rows: int32 [16, 2, 2], P('row', 'col'), may hold values from 0 to 0
- tile_cols: int32 [16, 2, 2], P('row', 'col'), may hold values from 0 to 7
- tile_counts: int32 [16, 2], P('row', 'col'), may hold values from 1 to 2, as said below
Outputs:
- basis: float32 [8192, 128], P(('row', 'col'))
- ritz: float32 [128, 128], replicated
Inputs may be any that keep to these rules, and one draw needn't show every extreme that they name: Slots 0 to tile_counts - 1 are live, the others are ignored.
All inputs are finite; a program needn't handle non-finite values.
Results may differ from a plain program's by a relative error of at most 0.0047.
The roundings to bfloat16 on the way count: a program that leaves them out, or rounds other values in their place, can miss the bound.
Values may be sent and summed in bfloat16 or wider, within the bound.
A program may use at most 64 MiB of HBM per device.

v0:
```python
import math

import jax
import jax.numpy as jnp
from jax import lax
from jax.sharding import PartitionSpec as P


def normalize(block_rows, gram_matrix, scale):
    factor = jnp.linalg.cholesky(gram_matrix)
    solved = lax.linalg.triangular_solve(
        factor, block_rows, left_side=False, lower=True, transpose_a=True
    )
    return scale * solved


def per_device(start_vectors, tiles, tile_rows, tile_cols, tile_counts):
    tile_set = tiles[0, 0]
    slot_rows = tile_rows[0, 0]
    slot_cols = tile_cols[0, 0]
    live_count = tile_counts[0, 0]
    piece_rows, width = start_vectors.shape
    slot_total = tile_set.shape[0]
    tile_size = tile_set.shape[-1]
    block_rows = lax.axis_size("col") * piece_rows
    block_tiles = block_rows // tile_size
    group_tiles = lax.axis_size("row") * piece_rows // tile_size
    scale = math.sqrt(lax.axis_size("row") * block_rows)
    vectors = start_vectors
    cross_terms = jnp.zeros((width, width), jnp.float32)
    for step in range(2):
        group = lax.all_gather(vectors.astype(jnp.bfloat16), "row", axis=0, tiled=True)
        picked = group.reshape(group_tiles, tile_size, width)[slot_cols]
        product = jnp.einsum("sij,sjk->sik", tile_set, picked, preferred_element_type=jnp.float32)
        slot_ids = jnp.arange(slot_total, dtype=jnp.int32)
        live = slot_ids < live_count
        targets = jnp.arange(block_tiles, dtype=jnp.int32)
        place = ((slot_rows[None, :] == targets[:, None]) & live[None, :]).astype(jnp.float32)
        summed = jnp.einsum("rs,sik->rik", place, product, precision=lax.Precision.HIGHEST)
        partial_value = summed.reshape(block_rows, width)
        mine = lax.psum_scatter(partial_value, "col", scatter_dimension=0, tiled=True)
        own_gram = jnp.dot(mine.T, mine, precision=lax.Precision.HIGHEST)
        if step == 0:
            gram_matrix = lax.psum(own_gram, ("row", "col"))
        else:
            own_cross = jnp.dot(vectors.T, mine, precision=lax.Precision.HIGHEST)
            gram_matrix, cross_terms = lax.psum((own_gram, own_cross), ("row", "col"))
        vectors = normalize(mine, gram_matrix, scale)
    ritz = cross_terms / scale
    return (vectors, ritz)


def solution(mesh):
    placed = (
        P(("row", "col"), None),
        P("row", "col", None, None, None),
        P("row", "col", None),
        P("row", "col", None),
        P("row", "col"),
    )
    return jax.shard_map(
        per_device,
        mesh=mesh,
        in_specs=placed,
        out_specs=(P(("row", "col"), None), P()),
        check_vma=False,
    )
```

profile of v0, /device:TPU:0, one launch (start us, length us, event | category | flops | bytes accessed | tf_op | source)
XLA Modules:
  0.0 461.1 jit_solution(2018740094089688186)
XLA Ops:
  7.2 0.0 copy-start
  7.2 0.0 all-gather.3.cloned.1.call-start
  7.2 1.6 convert_element_type.8
  8.8 0.0 all-gather.3.cloned.1.call-update
  8.9 0.0 copy-start.6
  8.9 0.0 reduce-scatter.3.cloned.1.call-start
  9.6 0.0 copy-done.6
  9.6 0.0 copy-start.7
  9.6 0.6 copy-done.7
  10.3 59.1 %all-gather.3.cloned.1.call-done = bf16[4096,128]{1,0:T(8,128)(2,1)} async-done(((bf16[256,128]{1,0:T(8,128)(2,1)}), bf16[4096,128]{1,0:T(8,128)(2,1)}) %all-gather.3.cloned.1.call-update) | async-done | bytes 1048592 | tf_op jit(solution)/shard_map/all_gather | solution.py:32
  69.4 1.8 gather_fusion
  71.2 0.0 copy-done
  71.2 0.5 convolution_bitcast_fusion.1
  71.7 0.2 copy.18
  71.9 1.8 fusion.15
  73.7 0.0 reduce-scatter.3.cloned.1.call-update
  73.7 0.0 all-reduce.4.cloned.1.call-start
  73.8 6.6 %reduce-scatter.3.cloned.1.call-done = f32[256,128]{1,0:T(8,128)} async-done(((f32[512,128]{1,0:T(8,128)}), f32[256,128]{1,0:T(8,128)}) %reduce-scatter.3.cloned.1.call-update) | async-done | bytes 131088 | tf_op jit(solution)/shard_map/reduce_scatter | solution.py:41
  80.3 2.0 fusion.16
  82.3 0.0 all-reduce.4.cloned.1.call-update
  82.4 0.0 all-gather.5.cloned.1.call-start
  82.4 123.7 %all-reduce.4.cloned.1.call-done = f32[128,128]{0,1:T(8,128)} async-done(((f32[128,128]{0,1:T(8,128)}), f32[128,128]{0,1:T(8,128)}) %all-reduce.4.cloned.1.call-update) | async-done | bytes 65552 | tf_op jit(solution)/shard_map/psum | solution.py:44
  206.1 0.0 copy-start.4
  206.1 1.0 copy.13
  207.1 0.0 copy-done.4
  207.2 0.0 copy-start.2
  207.2 11.7 %cholesky.44 = f32[128,128]{1,0:T(8,128)S(1)} custom-call(f32[128,128]{1,0:T(8,128)S(1)} %fusion.9), custom_call_target="Cholesky" | custom-call | tf_op jit(solution)/shard_map/jit(cholesky)/cholesky | solution.py:10
  218.9 0.6 compare_reduce_fusion.1
  219.6 0.7 fusion.4
  220.2 9.8 %custom-call.6 = f32[1,128,128]{1,2,0:T(8,128)S(1)} custom-call(f32[1,128,128]{2,1,0:T(8,128)S(1)} %fusion.4), custom_call_target="InvertDiagBlocksLowerTriangular" | custom-call | tf_op jit(solution)/shard_map/triangular_solve/custom-call.0 | solution.py:11
  230.0 0.0 copy-done.2
  230.1 0.9 fusion.14
  231.0 0.0 all-gather.5.cloned.1.call-update
  231.0 0.0 reduce-scatter.5.cloned.1.call-start
  231.1 56.0 %all-gather.5.cloned.1.call-done = bf16[4096,128]{0,1:T(8,128)(2,1)} async-done(((bf16[256,128]{0,1:T(8,128)(2,1)}), bf16[4096,128]{0,1:T(8,128)(2,1)}) %all-gather.5.cloned.1.call-update) | async-done | bytes 1048592 | tf_op jit(solution)/shard_map/all_gather | solution.py:32
  287.1 1.6 copy.24
  288.7 0.6 gather_fusion.1
  289.3 0.5 convolution_bitcast_fusion
  289.8 0.2 copy.21
  290.0 1.8 fusion.17
  291.8 0.0 reduce-scatter.5.cloned.1.call-update
  291.8 0.2 all-reduce.6.cloned.1.call-start
  292.1 6.4 %reduce-scatter.5.cloned.1.call-done = f32[256,128]{1,0:T(8,128)} async-done(((f32[512,128]{1,0:T(8,128)}), f32[256,128]{1,0:T(8,128)}) %reduce-scatter.5.cloned.1.call-update) | async-done | bytes 131088 | tf_op jit(solution)/shard_map/reduce_scatter | solution.py:41
  298.5 0.0 copy-start.1
  298.5 2.1 fusion.18
  300.6 0.0 copy-done.1
  300.6 0.9 fusion.19
  301.5 0.0 all-reduce.6.cloned.1.call-update
  301.5 127.1 %all-reduce.6.cloned.1.call-done = (f32[128,128]{0,1:T(8,128)}, f32[128,128]{1,0:T(8,128)}) async-done(((f32[128,128]{0,1:T(8,128)}, f32[128,128]{1,0:T(8,128)}), (f32[128,128]{0,1:T(8,128)}, f32[128,128]{1,0:T(8,128)})) %all-reduce.6.cloned.1.call-update) | async-done | bytes 131088 | tf_op jit(solution)/shard_map/psum | solution.py:47
  428.6 0.0 copy-start.3
  428.6 0.0 copy-start.5
  428.6 1.0 copy.16
  429.6 0.0 copy-done.3
  429.6 0.0 copy-done.5
  429.6 0.6 fusion.7
  430.3 11.7 %cholesky.55 = f32[128,128]{1,0:T(8,128)S(1)} custom-call(f32[128,128]{1,0:T(8,128)S(1)} %get-tuple-element.12), custom_call_target="Cholesky" | custom-call | tf_op jit(solution)/shard_map/jit(cholesky)/cholesky | solution.py:10
  442.0 0.6 compare_reduce_fusion
  442.7 0.7 fusion.5
  443.4 9.8 %custom-call.7 = f32[1,128,128]{1,2,0:T(8,128)S(1)} custom-call(f32[1,128,128]{2,1,0:T(8,128)S(1)} %fusion.5), custom_call_target="InvertDiagBlocksLowerTriangular" | custom-call | tf_op jit(solution)/shard_map/triangular_solve/custom-call.0 | solution.py:11
  453.2 0.3 fusion
  453.5 0.8 copy.17
  (6 shorter events, 0.1 us)
Async XLA Ops:
  7.2 64.0 %copy-start = (bf16[1,1,2,512,512]{4,3,2,1,0:T(8,128)(2,1)S(1)}, bf16[1,1,2,512,512]{4,3,2,1,0:T(8,128)(2,1)}, u32[]{:S(2)}) copy-start(bf16[1,1,2,512,512]{4,3,2,1,0:T(8,128)(2,1)} %param.9) | copy-start | bytes 3145732
  7.2 62.2 %all-gather.3.cloned.1.call-start = ((), (), s32[]{:S(2)}) async-start(), calls=%async_computation.2 | async-start | bytes 1114112 | tf_op jit(solution)/shard_map/all_gather | solution.py:32
  8.9 0.7 copy-start.6
  8.9 71.5 %reduce-scatter.3.cloned.1.call-start = ((), (), s32[]{:S(2)}) async-start(), calls=%async_computation.3 | async-start | bytes 393216 | tf_op jit(solution)/shard_map/reduce_scatter | solution.py:41
  9.6 0.7 copy-start.7
  73.7 132.4 %all-reduce.4.cloned.1.call-start = ((), (), s32[]{:S(2)}) async-start(), calls=%async_computation.4 | async-start | bytes 131072 | tf_op jit(solution)/shard_map/psum | solution.py:44
  82.4 204.7 %all-gather.5.cloned.1.call-start = ((), (), s32[]{:S(2)}) async-start(), calls=%async_computation.5 | async-start | bytes 1114112 | tf_op jit(solution)/shard_map/all_gather | solution.py:32
  206.1 1.0 copy-start.4
  207.2 22.9 %copy-start.2 = (f32[256,128]{1,0:T(8,128)S(1)}, f32[256,128]{1,0:T(8,128)}, u32[]{:S(2)}) copy-start(f32[256,128]{1,0:T(8,128)} %reduce-scatter.3.cloned.1.call-done) | copy-start | bytes 393220
  231.0 67.5 %reduce-scatter.5.cloned.1.call-start = ((), (), s32[]{:S(2)}) async-start(), calls=%async_computation.6 | async-start | bytes 393216 | tf_op jit(solution)/shard_map/reduce_scatter | solution.py:41
  291.8 136.8 %all-reduce.6.cloned.1.call-start = ((), (), s32[]{:S(2)}) async-start(), calls=%async_computation.7 | async-start | bytes 262144 | tf_op jit(solution)/shard_map/psum | solution.py:47
  298.5 2.1 copy-start.1
  428.6 1.0 copy-start.3
  428.6 1.0 copy-start.5
Sparse Core Ops, SparseCore 0:
  11.3 57.9 all-gather.2
  73.8 6.4 reduce-scatter.2
  87.4 118.6 all-reduce.3
  231.1 55.8 all-gather.4
  291.9 6.5 reduce-scatter.4
  304.6 123.9 all-reduce.5
where the time goes:
time: 461 us
  waiting for transfers between devices  379 us (82%)
  other arithmetic  48 us (10%)
  between operations  15 us (3%)
  matrix products  10.7 us (2%)
  local copies, waits for them, and re-layouts  7.92 us (2%)
    psum x1, waiting for transfers between devices, per_device(): gram_matrix, cross_terms = lax.psum((own_gram, own_cross), ('row', 'col'))  127 us
    psum x1, waiting for transfers between devices, per_device(): gram_matrix = lax.psum(own_gram, ('row', 'col'))  124 us
    all_gather x2, waiting for transfers between devices, per_device(): lax.all_gather(vectors.astype(jnp.bfloat16), 'row', axis=0, tiled=True)  115 us
    another operation x6, other arithmetic, normalize(): factor = jnp.linalg.cholesky(gram_matrix)  24.8 us
    another operation x4, other arithmetic, normalize(): lax.linalg.triangular_solve(factor, block_rows, left_side=False, lower=Tr...  20.9 us
    reduce_scatter x2, waiting for transfers between devices, per_device(): lax.psum_scatter(partial_value, 'col', scatter_dimension=0, tiled=True)  13 us
  transfers between devices with their start and end apart: 6, of which 6 were waited for; matrix products, arithmetic and copies ran while one was open for 0% of the time, Pallas kernels for 0%

commit v1 on v0

v1 whole, which is shorter than its diff:
```python
import functools
import math

import jax
import jax.numpy as jnp
from jax import lax
from jax.experimental import pallas as pl
from jax.experimental.pallas import tpu as pltpu
from jax.sharding import PartitionSpec as P

MESH = pl.DeviceIdType.MESH
HIGHEST = lax.Precision.HIGHEST
PANEL = 16


def dot_tn(left, right):
    return lax.dot_general(
        left, right, (((0,), (0,)), ((), ())), precision=HIGHEST,
        preferred_element_type=jnp.float32,
    )


def dot_nt(left, right):
    return lax.dot_general(
        left, right, (((1,), (1,)), ((), ())), precision=HIGHEST,
        preferred_element_type=jnp.float32,
    )


def invert_factor(gram, work, unit, inverse):
    width = gram.shape[0]
    rows = lax.broadcasted_iota(jnp.int32, (width, width), 0)
    lanes = lax.broadcasted_iota(jnp.int32, (width, width), 1)
    work[...] = gram
    unit[...] = jnp.where(rows == lanes, 1.0, 0.0)
    panel_rows = lax.broadcasted_iota(jnp.int32, (PANEL, width), 0)
    panel_lanes = lax.broadcasted_iota(jnp.int32, (PANEL, width), 1)
    for first in range(0, width, PANEL):
        last = first + PANEL
        left = work[first:last, :]
        right = unit[first:last, :]
        for i in range(PANEL):
            pivot_row = left[i : i + 1, :]
            pivot = pivot_row[:, first + i : first + i + 1]
            factor = left[:, first + i : first + i + 1] * (1.0 / pivot)
            factor = jnp.where(panel_rows > i, factor, 0.0)
            left = left - factor * pivot_row
            right = right - factor * right[i : i + 1, :]
        diagonal = jnp.where(panel_lanes == panel_rows + first, left, 0.0)
        diagonal = jnp.sum(diagonal, axis=1, keepdims=True)
        root = lax.rsqrt(diagonal)
        root = root * (1.5 - 0.5 * ((diagonal * root) * root))
        right = right * root
        inverse[first:last, :] = right
        if last < width:
            left = jnp.where(panel_lanes >= last, left * root, 0.0)
            change = dot_tn(left, left)
            work[last:, :] = work[last:, :] - change[last:, :]
            change = dot_tn(left, right)
            unit[last:, :] = unit[last:, :] - change[last:, :]


def kernel(
    n_row, n_col, inner,
    start_ref, tiles_ref, cols_ref, weights_ref,
    basis_ref, ritz_ref,
    group_first, group_second, parts, landed, grams, gathered, outers, finals, work, unit, inverse,
    near_send, near_recv, far_send, far_recv, part_send, part_recv,
    gram_send, gram_recv, outer_send, outer_recv, final_send, final_recv,
):
    outer = n_row // inner
    members = inner * n_col
    piece, width = start_ref.shape
    slots, tile = tiles_ref.shape[0], tiles_ref.shape[-1]
    chunk = width // members
    scale = math.sqrt(n_row * n_col * piece)
    row = lax.axis_index("row")
    col = lax.axis_index("col")
    out_index = lax.div(row, inner)
    in_index = lax.rem(row, inner)
    member = in_index * n_col + col

    def outer_peer(d):
        return lax.rem(out_index + d + outer, outer)

    def inner_peer(e):
        return lax.rem(in_index + e + inner, inner)

    def member_device(g):
        return (out_index * inner + lax.div(g, n_col), lax.rem(g, n_col))

    def remote(src, dst, send, recv, device):
        return pltpu.make_async_remote_copy(
            src_ref=src, dst_ref=dst, send_sem=send, recv_sem=recv,
            device_id=device, device_id_type=MESH,
        )

    barrier = pltpu.get_barrier_semaphore()
    for d in range(1, outer):
        pl.semaphore_signal(
            barrier, inc=1, device_id=(outer_peer(d) * inner + in_index, col),
            device_id_type=MESH,
        )
    for e in range(1, members):
        pl.semaphore_signal(
            barrier, inc=1, device_id=member_device(lax.rem(member + e, members)),
            device_id_type=MESH,
        )
    pl.semaphore_wait(barrier, outer - 1 + members - 1)

    def block_at(step, index):
        group = (group_first, group_second)[step]
        at = index * piece
        return group.at[lax.div(at, tile), pl.ds(pl.multiple_of(lax.rem(at, tile), piece), piece)]

    vectors = start_ref[...]
    for step in range(2):
        started = []
        total = step + 1

        def send(copy):
            copy.start()
            started.append(copy)

        own = block_at(step, row)
        own[...] = vectors.astype(jnp.bfloat16)
        for d in range(1, outer):
            send(remote(own, own, far_send.at[d], far_recv.at[d],
                        (outer_peer(d) * inner + in_index, col)))
        for d in range(outer):
            held = block_at(step, outer_peer(-d) * inner + in_index)
            if d > 0:
                remote(held, held, far_send.at[d], far_recv.at[d],
                       (outer_peer(-d) * inner + in_index, col)).wait_recv()
            for e in range(1, inner):
                send(remote(held, held, near_send.at[d * inner + e], near_recv.at[d * inner + e],
                            (out_index * inner + inner_peer(e), col)))
        for d in range(outer):
            for e in range(1, inner):
                came = block_at(step, outer_peer(-d) * inner + inner_peer(-e))
                remote(came, came, near_send.at[d * inner + e], near_recv.at[d * inner + e],
                       (out_index * inner + inner_peer(-e), col)).wait_recv()

        group = (group_first, group_second)[step]
        picked = [group[cols_ref[0, 0, s]] for s in range(slots)]
        for k in list(range(1, n_col)) + [0]:
            owner = lax.rem(col + k, n_col)
            at = owner * piece
            tile_row = lax.div(at, tile)
            offset = pl.multiple_of(lax.rem(at, tile), piece)
            value = jnp.zeros((piece, width), jnp.float32)
            for s in range(slots):
                product = jnp.dot(
                    tiles_ref[s, pl.ds(offset, piece), :], picked[s],
                    preferred_element_type=jnp.float32,
                )
                value = value + weights_ref[s, tile_row] * product
            if k > 0:
                parts[step, k] = value
                send(remote(parts.at[step, k], landed.at[step, col], part_send.at[k],
                            part_recv.at[k], (row, owner)))
            else:
                landed[step, col] = value
        for k in range(1, n_col):
            source = lax.rem(col - k + n_col, n_col)
            remote(parts.at[step, k], landed.at[step, source], part_send.at[k],
                   part_recv.at[k], (row, source)).wait_recv()
        mine = landed[step, 0]
        for c in range(1, n_col):
            mine = mine + landed[step, c]

        mats = [dot_tn(mine, mine)]
        if step == 1:
            mats.append(dot_tn(vectors, mine))
        for g in range(members):
            for m in range(total):
                grams[step, g, m * chunk : (m + 1) * chunk, :] = mats[m][g * chunk : (g + 1) * chunk, :]
        used_rows = pl.ds(0, total * chunk)
        for e in range(1, members):
            target = lax.rem(member + e, members)
            send(remote(grams.at[step, target, used_rows], gathered.at[step, e, used_rows],
                        gram_send.at[e], gram_recv.at[e], member_device(target)))
        sums = grams[step, member, 0 : total * chunk, :]
        for e in range(1, members):
            source = lax.rem(member - e + members, members)
            slot = gathered.at[step, e, used_rows]
            remote(slot, slot, gram_send.at[e], gram_recv.at[e], member_device(source)).wait_recv()
            sums = sums + gathered[step, e, 0 : total * chunk, :]
        own = outers.at[step, out_index, used_rows]
        own[...] = sums
        for d in range(1, outer):
            send(remote(own, own, outer_send.at[d], outer_recv.at[d],
                        (outer_peer(d) * inner + in_index, col)))
        for d in range(1, outer):
            came = outers.at[step, outer_peer(-d), used_rows]
            remote(came, came, outer_send.at[d], outer_recv.at[d],
                   (outer_peer(-d) * inner + in_index, col)).wait_recv()
        sums = outers[step, 0, 0 : total * chunk, :]
        for d in range(1, outer):
            sums = sums + outers[step, d, 0 : total * chunk, :]
        own = finals.at[step, member, used_rows]
        own[...] = sums
        for e in range(1, members):
            send(remote(own, own, final_send.at[e], final_recv.at[e],
                        member_device(lax.rem(member + e, members))))
        for e in range(1, members):
            source = lax.rem(member - e + members, members)
            came = finals.at[step, source, used_rows]
            remote(came, came, final_send.at[e], final_recv.at[e], member_device(source)).wait_recv()
        gram = jnp.concatenate([finals[step, g, 0:chunk, :] for g in range(members)], axis=0)
        if step == 1:
            for g in range(members):
                ritz_ref[g * chunk : (g + 1) * chunk, :] = finals[step, g, chunk : 2 * chunk, :] / scale

        invert_factor(gram, work, unit, inverse)
        vectors = scale * dot_nt(mine, inverse[...])
        for copy in started:
            copy.wait_send()
    basis_ref[...] = vectors


def per_device(n_row, n_col, start_vectors, tiles, tile_rows, tile_cols, tile_counts):
    piece, width = start_vectors.shape
    slots, tile = tiles.shape[2], tiles.shape[-1]
    targets = jnp.arange(n_col * piece // tile, dtype=jnp.int32)
    live = jnp.arange(slots, dtype=jnp.int32) < tile_counts[0, 0]
    placed = tile_rows[0, 0][:, None] == targets[None, :]
    weights = jnp.logical_and(placed, live[:, None]).astype(jnp.float32)
    inner = max(1, 8 // n_col)
    outer = n_row // inner
    members = inner * n_col
    chunk = width // members
    f32 = jnp.float32
    vmem = pl.BlockSpec(memory_space=pltpu.VMEM)
    smem = pl.BlockSpec(memory_space=pltpu.SMEM)
    dma = pltpu.SemaphoreType.DMA
    pairs = []
    for count in (outer * inner, outer, n_col, members, outer, members):
        pairs += [dma((count,)), dma((count,))]
    return pl.pallas_call(
        functools.partial(kernel, n_row, n_col, inner),
        out_shape=(
            jax.ShapeDtypeStruct((piece, width), f32),
            jax.ShapeDtypeStruct((width, width), f32),
        ),
        in_specs=[vmem, vmem, smem, smem],
        out_specs=(vmem, vmem),
        scratch_shapes=[
            pltpu.VMEM((n_row * piece // tile, tile, width), jnp.bfloat16),
            pltpu.VMEM((n_row * piece // tile, tile, width), jnp.bfloat16),
            pltpu.VMEM((2, n_col, piece, width), f32),
            pltpu.VMEM((2, n_col, piece, width), f32),
            pltpu.VMEM((2, members, 2 * chunk, width), f32),
            pltpu.VMEM((2, members, 2 * chunk, width), f32),
            pltpu.VMEM((2, outer, 2 * chunk, width), f32),
            pltpu.VMEM((2, members, 2 * chunk, width), f32),
            pltpu.VMEM((width, width), f32),
            pltpu.VMEM((width, width), f32),
            pltpu.VMEM((width, width), f32),
        ] + pairs,
        compiler_params=pltpu.CompilerParams(
            collective_id=0, has_side_effects=True, vmem_limit_bytes=40 * 1024 * 1024,
        ),
        name="krylov",
    )(start_vectors, tiles[0, 0], tile_cols, weights)


def solution(mesh):
    placed = (
        P(("row", "col"), None),
        P("row", "col", None, None, None),
        P("row", "col", None),
        P("row", "col", None),
        P("row", "col"),
    )
    return jax.shard_map(
        functools.partial(per_device, mesh.shape["row"], mesh.shape["col"]),
        mesh=mesh,
        in_specs=placed,
        out_specs=(P(("row", "col"), None), P()),
        check_vma=False,
    )
```

time: 461 us -> 90.3 us (0.20)
  waiting for transfers between devices: 379 us -> 0 us
  Pallas kernels: 0 us -> 84 us
  other arithmetic: 48 us -> 0.01 us
  between operations: 15 us -> 1.3 us
  matrix products: 10.7 us -> 0 us
    psum x2 -> x0, waiting for transfers between devices: 251 us -> none  [the longest x1 127 us: per_device(): gram_matrix, cross_terms = lax.psum((own_gram, own_cross), ('row', 'col'))]
    all_gather x2 -> x0, waiting for transfers between devices: 115 us -> none  [per_device(): lax.all_gather(vectors.astype(jnp.bfloat16), 'row', axis=0, tiled=True)]
    pallas_call x0 -> x1, Pallas kernels: none -> 84 us  [per_device(): pl.pallas_call(functools.partial(kernel, n_row, n_col, inner), out_shape=...]
    another operation x10 -> x0, other arithmetic: 45.7 us -> none  [the longest x6 24.8 us: normalize(): factor = jnp.linalg.cholesky(gram_matrix)]
    reduce_scatter x2 -> x0, waiting for transfers between devices: 13 us -> none  [per_device(): lax.psum_scatter(partial_value, 'col', scatter_dimension=0, tiled=True)]
    dot_general x7 -> x0, matrix products: 9.46 us -> none  [the longest x2 4.06 us: per_device(): own_gram = jnp.dot(mine.T, mine, precision=lax.Precision.HIGHEST)]
  transfers between devices with their start and end apart: 6 -> 0, of which waited for: 6 -> 0; matrix products, arithmetic and copies ran while one was open for 0% -> 0% of each run, Pallas kernels for 0% -> 0%
where the time goes in v1:
time: 90.3 us; the launch traced here: 90.1 us
  Pallas kernels  84 us (93%)
  local copies, waits for them, and re-layouts  4.82 us (5%)
  between operations  1.3 us (1%)
    pallas_call x1, Pallas kernels, per_device(): pl.pallas_call(functools.partial(kernel, n_row, n_col, inner), out_shape=...  84 us
    unnamed x10, local copies, waits for them, and re-layouts  4.71 us

profile of v1, /device:TPU:0, one launch (start us, length us, event | category | flops | bytes accessed | tf_op | source)
XLA Modules:
  0.0 90.1 jit_solution(8648489166144287445)
XLA Ops:
  1.3 0.0 copy-start.3
  1.3 0.6 copy-done.3
  1.9 0.1 copy.7
  2.0 0.0 copy-start.2
  2.1 0.6 copy-done.2
  2.7 0.0 copy-start
  2.7 1.2 %copy-done = bf16[1,1,2,512,512]{4,3,2,1,0:T(8,128)(2,1)S(1)} copy-done((bf16[1,1,2,512,512]{4,3,2,1,0:T(8,128)(2,1)S(1)}, bf16[1,1,2,512,512]{4,3,2,1,0:T(8,128)(2,1)}, u32[]{:S(2)}) %copy-start) | copy-done | bytes 1048600
  3.9 0.0 copy-start.1
  3.9 0.9 %copy-done.1 = f32[256,128]{1,0:T(8,128)S(1)} copy-done((f32[256,128]{1,0:T(8,128)S(1)}, f32[256,128]{1,0:T(8,128)}, u32[]{:S(2)}) %copy-start.1) | copy-done | bytes 131096
  4.8 84.0 %krylov.1 = (f32[256,128]{1,0:T(8,128)S(1)}, f32[128,128]{1,0:T(8,128)S(1)}) custom-call(f32[256,128]{1,0:T(8,128)S(1)} %copy-done.1, bf16[2,512,512]{2,1,0:T(8,128)(2,1)S(1)} %bitcast.5, s32[1,1,2]{2,1,0:T(1,128)S(1)} %copy-done.2, f32[2,1]{1,0:T(2,128)S(1)} %and_convert_fusion.weights_ref), custom_call_target="tpu_custom_call" | custom-call | tf_op jit(solution)/shard_map/krylov/pallas_call | solution.py:240
  88.8 0.7 copy.11
  89.5 0.6 copy.12
  (2 shorter events, 0.0 us)
Async XLA Ops:
  1.3 0.7 copy-start.3
  2.0 0.7 copy-start.2
  2.7 1.2 %copy-start = (bf16[1,1,2,512,512]{4,3,2,1,0:T(8,128)(2,1)S(1)}, bf16[1,1,2,512,512]{4,3,2,1,0:T(8,128)(2,1)}, u32[]{:S(2)}) copy-start(bf16[1,1,2,512,512]{4,3,2,1,0:T(8,128)(2,1)} %param.6) | copy-start | bytes 3145732
  3.9 0.9 %copy-start.1 = (f32[256,128]{1,0:T(8,128)S(1)}, f32[256,128]{1,0:T(8,128)}, u32[]{:S(2)}) copy-start(f32[256,128]{1,0:T(8,128)} %start_ref.1) | copy-start | bytes 393220

commit v2 on v1

--- a/solution.py
+++ b/solution.py
@@ -39,15 +39,22 @@
         last = first + PANEL
         left = work[first:last, :]
         right = unit[first:last, :]
+        spread = [
+            jnp.broadcast_to(left[:, first + k : first + k + 1], (PANEL, width))
+            for k in range(PANEL)
+        ]
+        diagonal = spread[0]
         for i in range(PANEL):
-            pivot_row = left[i : i + 1, :]
-            pivot = pivot_row[:, first + i : first + i + 1]
-            factor = left[:, first + i : first + i + 1] * (1.0 / pivot)
-            factor = jnp.where(panel_rows > i, factor, 0.0)
-            left = left - factor * pivot_row
+            column = spread[i]
+            if i > 0:
+                diagonal = jnp.where(panel_rows == i, column, diagonal)
+            if i == PANEL - 1:
+                break
+            factor = jnp.where(panel_rows > i, column * (1.0 / column[i : i + 1, :]), 0.0)
+            for k in range(i + 1, PANEL):
+                spread[k] = spread[k] - factor * spread[k][i : i + 1, :]
+            left = left - factor * left[i : i + 1, :]
             right = right - factor * right[i : i + 1, :]
-        diagonal = jnp.where(panel_lanes == panel_rows + first, left, 0.0)
-        diagonal = jnp.sum(diagonal, axis=1, keepdims=True)
         root = lax.rsqrt(diagonal)
         root = root * (1.5 - 0.5 * ((diagonal * root) * root))
         right = right * root
@@ -62,9 +69,10 @@
 
 def kernel(
     n_row, n_col, inner,
-    start_ref, tiles_ref, cols_ref, weights_ref,
+    start_ref, tiles_hbm, cols_ref, weights_ref,
     basis_ref, ritz_ref,
     group_first, group_second, parts, landed, grams, gathered, outers, finals, work, unit, inverse,
+    tiles_ref, tiles_sem,
     near_send, near_recv, far_send, far_recv, part_send, part_recv,
     gram_send, gram_recv, outer_send, outer_recv, final_send, final_recv,
 ):
@@ -95,6 +103,8 @@
             device_id=device, device_id_type=MESH,
         )
 
+    loading = pltpu.make_async_copy(tiles_hbm, tiles_ref, tiles_sem)
+    loading.start()
     barrier = pltpu.get_barrier_semaphore()
     for d in range(1, outer):
         pl.semaphore_signal(
@@ -142,6 +152,8 @@
                        (out_index * inner + inner_peer(-e), col)).wait_recv()
 
         group = (group_first, group_second)[step]
+        if step == 0:
+            loading.wait()
         picked = [group[cols_ref[0, 0, s]] for s in range(slots)]
         for k in list(range(1, n_col)) + [0]:
             owner = lax.rem(col + k, n_col)
@@ -243,7 +255,7 @@
             jax.ShapeDtypeStruct((piece, width), f32),
             jax.ShapeDtypeStruct((width, width), f32),
         ),
-        in_specs=[vmem, vmem, smem, smem],
+        in_specs=[vmem, pl.BlockSpec(memory_space=pl.ANY), smem, smem],
         out_specs=(vmem, vmem),
         scratch_shapes=[
             pltpu.VMEM((n_row * piece // tile, tile, width), jnp.bfloat16),
@@ -257,6 +269,8 @@
             pltpu.VMEM((width, width), f32),
             pltpu.VMEM((width, width), f32),
             pltpu.VMEM((width, width), f32),
+            pltpu.VMEM(tiles.shape[2:], tiles.dtype),
+            dma(()),
         ] + pairs,
         compiler_params=pltpu.CompilerParams(
             collective_id=0, has_side_effects=True, vmem_limit_bytes=40 * 1024 * 1024,

time: 90.3 us -> 74.5 us (0.83)
  Pallas kernels: 84 us -> 68.1 us
    pallas_call x1, Pallas kernels: 84 us -> 68.1 us  [per_device(): pl.pallas_call(functools.partial(kernel, n_row, n_col, inner), out_shape=...]
where the time goes in v2:
time: 74.5 us; the launch traced here: 74.3 us
  Pallas kernels  68.1 us (91%)
  local copies, waits for them, and re-layouts  4.82 us (6%)
  between operations  1.3 us (2%)
    pallas_call x1, Pallas kernels, per_device(): pl.pallas_call(functools.partial(kernel, n_row, n_col, inner), out_shape=...  68.1 us
    unnamed x10, local copies, waits for them, and re-layouts  4.71 us

profile of v2, /device:TPU:0, one launch (start us, length us, event | category | flops | bytes accessed | tf_op | source)
XLA Modules:
  0.0 74.3 jit_solution(410860502118721292)
XLA Ops:
  1.3 0.0 copy-start.3
  1.3 0.6 copy-done.3
  1.9 0.1 copy.7
  2.0 0.0 copy-start.2
  2.1 0.6 copy-done.2
  2.7 0.0 copy-start
  2.7 1.2 %copy-done = bf16[1,1,2,512,512]{4,3,2,1,0:T(8,128)(2,1)S(1)} copy-done((bf16[1,1,2,512,512]{4,3,2,1,0:T(8,128)(2,1)S(1)}, bf16[1,1,2,512,512]{4,3,2,1,0:T(8,128)(2,1)}, u32[]{:S(2)}) %copy-start) | copy-done | bytes 1048600
  3.9 0.0 copy-start.1
  3.9 0.9 %copy-done.1 = f32[256,128]{1,0:T(8,128)S(1)} copy-done((f32[256,128]{1,0:T(8,128)S(1)}, f32[256,128]{1,0:T(8,128)}, u32[]{:S(2)}) %copy-start.1) | copy-done | bytes 131096
  4.8 68.1 %krylov.1 = (f32[256,128]{1,0:T(8,128)S(1)}, f32[128,128]{1,0:T(8,128)S(1)}) custom-call(f32[256,128]{1,0:T(8,128)S(1)} %copy-done.1, bf16[2,512,512]{2,1,0:T(8,128)(2,1)S(1)} %bitcast.5, s32[1,1,2]{2,1,0:T(1,128)S(1)} %copy-done.2, f32[2,1]{1,0:T(2,128)S(1)} %and_convert_fusion.weights_ref), custom_call_target="tpu_custom_call" | custom-call | tf_op jit(solution)/shard_map/krylov/pallas_call | solution.py:252
  73.0 0.7 copy.11
  73.6 0.6 copy.12
  (2 shorter events, 0.0 us)
Async XLA Ops:
  1.3 0.7 copy-start.3
  2.0 0.7 copy-start.2
  2.7 1.2 %copy-start = (bf16[1,1,2,512,512]{4,3,2,1,0:T(8,128)(2,1)S(1)}, bf16[1,1,2,512,512]{4,3,2,1,0:T(8,128)(2,1)}, u32[]{:S(2)}) copy-start(bf16[1,1,2,512,512]{4,3,2,1,0:T(8,128)(2,1)} %param.6) | copy-start | bytes 3145732
  3.9 0.9 %copy-start.1 = (f32[256,128]{1,0:T(8,128)S(1)}, f32[256,128]{1,0:T(8,128)}, u32[]{:S(2)}) copy-start(f32[256,128]{1,0:T(8,128)} %start_ref.1) | copy-start | bytes 393220

commit v3 on v2

--- a/solution.py
+++ b/solution.py
@@ -10,7 +10,7 @@
 
 MESH = pl.DeviceIdType.MESH
 HIGHEST = lax.Precision.HIGHEST
-PANEL = 16
+PANEL = 32
 
 
 def dot_tn(left, right):
@@ -69,10 +69,10 @@
 
 def kernel(
     n_row, n_col, inner,
-    start_ref, tiles_hbm, cols_ref, weights_ref,
+    start_hbm, tiles_hbm, rows_ref, cols_ref, counts_ref,
     basis_ref, ritz_ref,
     group_first, group_second, parts, landed, grams, gathered, outers, finals, work, unit, inverse,
-    tiles_ref, tiles_sem,
+    tiles_ref, start_ref, tiles_sem, start_sem,
     near_send, near_recv, far_send, far_recv, part_send, part_recv,
     gram_send, gram_recv, outer_send, outer_recv, final_send, final_recv,
 ):
@@ -104,6 +104,8 @@
         )
 
     loading = pltpu.make_async_copy(tiles_hbm, tiles_ref, tiles_sem)
+    starting = pltpu.make_async_copy(start_hbm, start_ref, start_sem)
+    starting.start()
     loading.start()
     barrier = pltpu.get_barrier_semaphore()
     for d in range(1, outer):
@@ -123,6 +125,7 @@
         at = index * piece
         return group.at[lax.div(at, tile), pl.ds(pl.multiple_of(lax.rem(at, tile), piece), piece)]
 
+    starting.wait()
     vectors = start_ref[...]
     for step in range(2):
         started = []
@@ -162,11 +165,13 @@
             offset = pl.multiple_of(lax.rem(at, tile), piece)
             value = jnp.zeros((piece, width), jnp.float32)
             for s in range(slots):
+                apart = rows_ref[0, 0, s] - tile_row
+                weight = jnp.maximum(1 - apart * apart, 0) * jnp.minimum(jnp.maximum(counts_ref[0, 0] - s, 0), 1)
                 product = jnp.dot(
                     tiles_ref[s, pl.ds(offset, piece), :], picked[s],
                     preferred_element_type=jnp.float32,
                 )
-                value = value + weights_ref[s, tile_row] * product
+                value = value + weight.astype(jnp.float32) * product
             if k > 0:
                 parts[step, k] = value
                 send(remote(parts.at[step, k], landed.at[step, col], part_send.at[k],
@@ -233,17 +238,14 @@
 
 def per_device(n_row, n_col, start_vectors, tiles, tile_rows, tile_cols, tile_counts):
     piece, width = start_vectors.shape
-    slots, tile = tiles.shape[2], tiles.shape[-1]
-    targets = jnp.arange(n_col * piece // tile, dtype=jnp.int32)
-    live = jnp.arange(slots, dtype=jnp.int32) < tile_counts[0, 0]
-    placed = tile_rows[0, 0][:, None] == targets[None, :]
-    weights = jnp.logical_and(placed, live[:, None]).astype(jnp.float32)
+    tile = tiles.shape[-1]
     inner = max(1, 8 // n_col)
     outer = n_row // inner
     members = inner * n_col
     chunk = width // members
     f32 = jnp.float32
     vmem = pl.BlockSpec(memory_space=pltpu.VMEM)
+    hbm = pl.BlockSpec(memory_space=pl.ANY)
     smem = pl.BlockSpec(memory_space=pltpu.SMEM)
     dma = pltpu.SemaphoreType.DMA
     pairs = []
@@ -255,7 +257,7 @@
             jax.ShapeDtypeStruct((piece, width), f32),
             jax.ShapeDtypeStruct((width, width), f32),
         ),
-        in_specs=[vmem, pl.BlockSpec(memory_space=pl.ANY), smem, smem],
+        in_specs=[hbm, hbm, smem, smem, smem],
         out_specs=(vmem, vmem),
         scratch_shapes=[
             pltpu.VMEM((n_row * piece // tile, tile, width), jnp.bfloat16),
@@ -270,13 +272,15 @@
             pltpu.VMEM((width, width), f32),
             pltpu.VMEM((width, width), f32),
             pltpu.VMEM(tiles.shape[2:], tiles.dtype),
+            pltpu.VMEM((piece, width), f32),
+            dma(()),
             dma(()),
         ] + pairs,
         compiler_params=pltpu.CompilerParams(
-            collective_id=0, has_side_effects=True, vmem_limit_bytes=40 * 1024 * 1024,
+            collective_id=0, has_side_effects=True, vmem_limit_bytes=60 * 1024 * 1024,
         ),
         name="krylov",
-    )(start_vectors, tiles[0, 0], tile_cols, weights)
+    )(start_vectors, tiles[0, 0], tile_rows, tile_cols, tile_counts)
 
 
 def solution(mesh):

time: 74.5 us -> 71.8 us (0.964)
  local copies, waits for them, and re-layouts: 4.82 us -> 2.23 us
    unnamed x10 -> x4, local copies, waits for them, and re-layouts: 4.71 us -> 2.23 us
where the time goes in v3:
time: 71.8 us; the launch traced here: 71.7 us
  Pallas kernels  68.1 us (95%)
  local copies, waits for them, and re-layouts  2.23 us (3%)
  between operations  1.29 us (2%)
    pallas_call x1, Pallas kernels, per_device(): pl.pallas_call(functools.partial(kernel, n_row, n_col, inner), out_shape=...  68.1 us
    unnamed x4, local copies, waits for them, and re-layouts  2.23 us

profile of v3, /device:TPU:0, one launch (start us, length us, event | category | flops | bytes accessed | tf_op | source)
XLA Modules:
  0.0 71.7 jit_solution(1439839715644559428)
XLA Ops:
  1.3 68.1 %krylov.1 = (f32[256,128]{1,0:T(8,128)}, f32[128,128]{1,0:T(8,128)}) custom-call(f32[256,128]{1,0:T(8,128)} %start_hbm.1, bf16[2,512,512]{2,1,0:T(8,128)(2,1)} %bitcast.1, s32[1,1,2]{2,1,0:T(1,128)} %rows_ref.1, s32[1,1,2]{2,1,0:T(1,128)} %cols_ref.1, s32[1,1]{1,0:T(1,128)S(6)} %copy.9.counts_ref), custom_call_target="tpu_custom_call" | custom-call | tf_op jit(solution)/shard_map/krylov/pallas_call | solution.py:254
  69.4 0.0 copy-start
  69.4 1.6 %copy.10 = f32[256,128]{1,0:T(8,128)} copy(f32[256,128]{1,0:T(8,128)} %get-tuple-element.4) | data formatting | bytes 262144
  71.0 0.0 copy-done
  71.0 0.6 copy.11
Async XLA Ops:
  69.4 1.6 %copy-start = (f32[128,128]{1,0:T(8,128)S(1)}, f32[128,128]{1,0:T(8,128)}, u32[]{:S(2)}) copy-start(f32[128,128]{1,0:T(8,128)} %get-tuple-element.5) | copy-start | bytes 196612
